TPU v7x, 512 devices: a whole 4x4x16 slice. The times are simulated.
512 devices in a mesh: seq: 8 (over y, core), fsdp: 16 (over z), dp: 4 (over x).
Axes of the slice: x: 4, y: 4, z: 16, core: 2. Of those that a mesh axis runs over, the one named last changes fastest.
Arguments:
- query_in: bfloat16 [64, 1024, 1536], P(('fsdp', 'dp'), 'seq'), may hold values from -8 to 8
- key_in: bfloat16 [64, 1024, 1536], P(('fsdp', 'dp'), 'seq'), may hold values from -8 to 8
- value_in: bfloat16 [64, 1024, 1536], P(('fsdp', 'dp'), 'seq'), may hold values from -24 to 24
- out_grad: bfloat16 [64, 1024, 1536], P(('fsdp', 'dp'), 'seq'), may hold values from -16 to 16
- out_weight: bfloat16 [1536, 1536], P('seq', 'fsdp'), may hold values from -0.15625 to 0.15625
- key_tiles: int32 [64, 24, 32, 6], P(('fsdp', 'dp'), 'seq'), may hold values from 0 to 31, as said below
- key_count: int32 [64, 24, 32], P(('fsdp', 'dp'), 'seq'), may hold values from 1 to 6, as said below
Outputs:
- layer_out: bfloat16 [64, 1024, 1536], P(('fsdp', 'dp'), 'seq')
- query_grad: bfloat16 [64, 1024, 1536], P(('fsdp', 'dp'), 'seq')
- key_grad: bfloat16 [64, 1024, 1536], P(('fsdp', 'dp'), 'seq')
- value_grad: bfloat16 [64, 1024, 1536], P(('fsdp', 'dp'), 'seq')
- weight_grad: float32 [1536, 1536], P('seq', ('fsdp', 'dp'))
Inputs may be any that keep to these rules, and one draw needn't show every extreme that they name: Tile m lies in frame m // 2, row (m) % 2 and column m % 1 of a grid of 16 frames. The first key_count[c, h, n] entries of key_tiles[c, h, n, :] are, in some order, the distinct tiles whose frame, row and column differ from those of tile n by at most the frame, row and column reach of head h in clip c, each 0 or 1; the remaining entries are arbitrary tile numbers. `key_count`: the number of live entries of each list; every clip has a list with 6.
All inputs are finite; a program needn't handle non-finite values.
Results may differ from a plain program's by a relative error of at most 0.02.
Values may be sent and summed in bfloat16 or wider, within the bound.
No kernel may reach another device: no remote copies, remote signals or barrier semaphores. Data moves between devices by JAX's collectives and lax.ppermute only.
A program may use at most 128 MiB of HBM per device.

v0:
```python
import jax
import jax.numpy as jnp
from jax import lax
from jax.sharding import PartitionSpec as P


def head_forward(query_head, key_head, value_head, head_list, tile_counts):
    tile_number, tile_len, head_dim = query_head.shape
    slot_number = head_list.shape[1]
    score_scale = head_dim ** (-0.5)
    key_chosen = key_head[head_list].reshape(tile_number, slot_number * tile_len, head_dim)
    value_chosen = value_head[head_list].reshape(tile_number, slot_number * tile_len, head_dim)
    kept_mask = (jnp.arange(slot_number * tile_len) // tile_len)[None, :] < tile_counts[:, None]
    scores = (
        jnp.einsum("nqd,nkd->nqk", query_head, key_chosen, preferred_element_type=jnp.float32)
        * score_scale
    )
    scores = jnp.where(kept_mask[:, None, :], scores, -jnp.inf)
    row_max = jnp.max(scores, axis=-1, keepdims=True)
    log_total = row_max + jnp.log(jnp.sum(jnp.exp(scores - row_max), axis=-1, keepdims=True))
    rounded = jnp.exp(scores - log_total).astype(jnp.bfloat16)
    attended = jnp.einsum(
        "nqk,nkd->nqd", rounded, value_chosen, preferred_element_type=jnp.float32
    ).astype(jnp.bfloat16)
    return (attended, log_total)


def head_backward(
    query_head, key_head, value_head, head_list, tile_counts, attended, log_total, upstream
):
    tile_number, tile_len, head_dim = query_head.shape
    slot_number = head_list.shape[1]
    score_scale = head_dim ** (-0.5)
    key_chosen = key_head[head_list].reshape(tile_number, slot_number * tile_len, head_dim)
    value_chosen = value_head[head_list].reshape(tile_number, slot_number * tile_len, head_dim)
    kept_mask = (jnp.arange(slot_number * tile_len) // tile_len)[None, :] < tile_counts[:, None]
    scores = (
        jnp.einsum("nqd,nkd->nqk", query_head, key_chosen, preferred_element_type=jnp.float32)
        * score_scale
    )
    scores = jnp.where(kept_mask[:, None, :], scores, -jnp.inf)
    weights = jnp.exp(scores - log_total)
    rounded = weights.astype(jnp.bfloat16)
    inner_sum = jnp.sum(
        upstream.astype(jnp.float32) * attended.astype(jnp.float32), axis=-1, keepdims=True
    )
    prob_grad = jnp.einsum(
        "nqd,nkd->nqk", upstream, value_chosen, preferred_element_type=jnp.float32
    )
    score_grad = (weights * (prob_grad - inner_sum)).astype(jnp.bfloat16)
    query_grad = (
        jnp.einsum("nqk,nkd->nqd", score_grad, key_chosen, preferred_element_type=jnp.float32)
        * score_scale
    ).astype(jnp.bfloat16)
    key_slots = (
        jnp.einsum("nqk,nqd->nkd", score_grad, query_head, preferred_element_type=jnp.float32)
        * score_scale
    )
    value_slots = jnp.einsum("nqk,nqd->nkd", rounded, upstream, preferred_element_type=jnp.float32)
    live_slots = jnp.arange(slot_number)[None, :] < tile_counts[:, None]
    one_hot = (
        (head_list[:, :, None] == jnp.arange(tile_number)[None, None, :]) & live_slots[:, :, None]
    ).astype(jnp.float32)
    slot_shape = (tile_number, slot_number, tile_len, head_dim)
    key_grad = jnp.einsum(
        "nst,nsrd->trd", one_hot, key_slots.reshape(slot_shape), precision=lax.Precision.HIGHEST
    ).astype(jnp.bfloat16)
    value_grad = jnp.einsum(
        "nst,nsrd->trd", one_hot, value_slots.reshape(slot_shape), precision=lax.Precision.HIGHEST
    ).astype(jnp.bfloat16)
    return (query_grad, key_grad, value_grad)


def heads_to_rows(stacked):
    return jnp.transpose(stacked, (1, 2, 0, 3)).reshape(
        stacked.shape[1] * stacked.shape[2], stacked.shape[0] * stacked.shape[3]
    )


def pick_head(field, head_index):
    return lax.dynamic_index_in_dim(field, head_index, 2, keepdims=False)


def per_device(query_in, key_in, value_in, out_grad, out_weight, key_tiles, key_count):
    seq_size = lax.axis_size("seq")
    fsdp_size = lax.axis_size("fsdp")
    local_tokens = query_in.shape[1]
    query_heads, key_heads, value_heads = (
        lax.all_to_all(query_in[0], "seq", split_axis=1, concat_axis=0, tiled=True),
        lax.all_to_all(key_in[0], "seq", split_axis=1, concat_axis=0, tiled=True),
        lax.all_to_all(value_in[0], "seq", split_axis=1, concat_axis=0, tiled=True),
    )
    clip_lists = key_tiles[0]
    clip_counts = key_count[0]
    local_heads, tile_number, slot_number = clip_lists.shape
    all_tokens = query_heads.shape[0]
    tile_len = all_tokens // tile_number
    head_dim = query_heads.shape[1] // local_heads
    grid_shape = (tile_number, tile_len, local_heads, head_dim)
    query_grid = query_heads.reshape(grid_shape)
    key_grid = key_heads.reshape(grid_shape)
    value_grid = value_heads.reshape(grid_shape)

    def forward_head(head_index):
        return head_forward(
            pick_head(query_grid, head_index),
            pick_head(key_grid, head_index),
            pick_head(value_grid, head_index),
            clip_lists[head_index],
            clip_counts[head_index],
        )

    attended, log_total = lax.map(forward_head, jnp.arange(local_heads))
    attn_heads = heads_to_rows(attended)
    attn_tokens = lax.all_to_all(attn_heads, "seq", split_axis=0, concat_axis=1, tiled=True)
    row_block, col_block = out_weight.shape
    gathered = lax.all_gather(out_weight[None], ("seq", "fsdp"), axis=0, tiled=True)
    full_weight = gathered.reshape(seq_size, fsdp_size, row_block, col_block)
    weight_code = "sfrc"
    attn_split = attn_tokens.reshape(local_tokens, seq_size, row_block)
    layer_out = jnp.einsum(
        "tsr," + weight_code + "->tfc", attn_split, full_weight, preferred_element_type=jnp.float32
    )
    layer_out = layer_out.reshape(local_tokens, fsdp_size * col_block).astype(jnp.bfloat16)
    grad_all = lax.all_gather(out_grad[0], "seq", axis=0, tiled=True)
    grad_split = out_grad[0].reshape(local_tokens, fsdp_size, col_block)
    upstream_tokens = jnp.einsum(
        "tfc," + weight_code + "->tsr", grad_split, full_weight, preferred_element_type=jnp.float32
    )
    upstream_tokens = upstream_tokens.reshape(local_tokens, seq_size * row_block).astype(
        jnp.bfloat16
    )
    upstream = lax.all_to_all(upstream_tokens, "seq", split_axis=1, concat_axis=0, tiled=True)
    upstream_grid = upstream.reshape(grid_shape)

    def backward_head(head_index):
        return head_backward(
            pick_head(query_grid, head_index),
            pick_head(key_grid, head_index),
            pick_head(value_grid, head_index),
            clip_lists[head_index],
            clip_counts[head_index],
            attended[head_index],
            log_total[head_index],
            pick_head(upstream_grid, head_index),
        )

    query_back, key_back, value_back = lax.map(backward_head, jnp.arange(local_heads))
    query_grad, key_grad, value_grad = (
        lax.all_to_all(heads_to_rows(query_back), "seq", split_axis=0, concat_axis=1, tiled=True),
        lax.all_to_all(heads_to_rows(key_back), "seq", split_axis=0, concat_axis=1, tiled=True),
        lax.all_to_all(heads_to_rows(value_back), "seq", split_axis=0, concat_axis=1, tiled=True),
    )
    weight_term = lax.dot_general(
        attn_heads, grad_all, (((0,), (0,)), ((), ())), preferred_element_type=jnp.float32
    )
    weight_part = lax.psum_scatter(weight_term, ("fsdp", "dp"), scatter_dimension=1, tiled=True)
    weight_grad = weight_part / (fsdp_size * lax.axis_size("dp"))
    return (layer_out[None], query_grad[None], key_grad[None], value_grad[None], weight_grad)


def solution(mesh):
    placed = (
        P(("fsdp", "dp"), "seq", None),
        P(("fsdp", "dp"), "seq", None),
        P(("fsdp", "dp"), "seq", None),
        P(("fsdp", "dp"), "seq", None),
        P("seq", "fsdp"),
        P(("fsdp", "dp"), "seq", None, None),
        P(("fsdp", "dp"), "seq", None),
    )
    return jax.shard_map(
        per_device,
        mesh=mesh,
        in_specs=placed,
        out_specs=(
            P(("fsdp", "dp"), "seq", None),
            P(("fsdp", "dp"), "seq", None),
            P(("fsdp", "dp"), "seq", None),
            P(("fsdp", "dp"), "seq", None),
            P("seq", ("fsdp", "dp")),
        ),
        check_vma=False,
    )
```

profile of v0, /device:TPU:1, one launch (start us, length us, event | category | flops | bytes accessed | tf_op | source)
XLA Modules:
  0.0 940.7 jit_solution(14607773695680848863)
XLA Ops:
  7.9 2.0 copy.158
  9.9 10.2 %all-to-all-start = ((bf16[128,8,192]{0,2,1:T(8,128)(2,1)}), bf16[128,8,192]{0,2,1:T(8,128)(2,1)S(1)}, u32[]{:S(2)}, u32[]{:S(2)}) async-start(bf16[128,8,192]{0,2,1:T(8,128)(2,1)} %bitcast.31), calls=%async_computation | async-start | bytes 786432 | tf_op jit(solution)/shard_map/all_to_all | solution.py:89
  21.0 7.2 all-to-all-done
  28.2 4.2 all-to-all-start.1
  33.4 7.6 all-to-all-done.1
  41.0 4.1 all-to-all-start.2
  50.0 3.2 all-to-all-done.2
  55.9 31.0 %while.30 = (s32[]{:T(128)}, bf16[3,32,32,64]{3,2,1,0:T(8,128)(2,1)}, f32[3,32,32,1]{2,1,3,0:T(8,128)}, s32[3]{0:T(128)S(1)}, s32[3,32]{1,0:T(4,128)S(1)}, /*ind...) while((s32[]{:T(128)}, ...), condition=%wide.region_3.4_spmd, body=%wide.region_0.3_spmd.sunk | while | flops 51781700 | bytes 8198467 | solution.py:113
  61.6 2.1 fusion.118
  64.8 1.5 fusion.119
  72.0 2.1 fusion.118
  75.1 1.5 fusion.119
  82.3 2.1 fusion.118
  85.4 1.5 fusion.119
  86.9 1.8 copy.168
  91.0 70.4 %all-gather.5.cloned.1.call-done = bf16[24576,96]{1,0:T(8,128)(2,1)} async-done(((bf16[192,96]{1,0:T(8,128)(2,1)}), bf16[24576,96]{1,0:T(8,128)(2,1)}) %all-gather.5.cloned.1.call-update) | async-done | bytes 4718608 | tf_op jit(solution)/shard_map/all_gather | solution.py:117
  161.5 9.4 copy.172
  170.8 10.7 %dot_general.75 = bf16[1536,96,16]{0,1,2:T(8,128)(2,1)} reshape(bf16[8,192,96,16]{1,0,2,3:T(8,128)(2,1)} %bitcast.247) | data formatting | bytes 9437184 | tf_op jit(solution)/shard_map/tfc,sfrc->tsr/dot_general | solution.py:127
  181.5 3.3 fusion.71
  185.7 3.6 all-to-all-start.4
  189.3 4.7 all-gather.7.cloned.1.call-done
  194.0 4.4 fusion.68
  198.5 3.9 all-to-all-start.3
  205.0 89.6 %while.31 = (s32[]{:T(128)}, bf16[3,32,32,64]{3,2,1,0:T(8,128)(2,1)}, bf16[3,32,32,64]{3,1,2,0:T(8,128)(2,1)}, bf16[3,32,32,64]{3,1,2,0:T(8,128)(2,1)}, s32[3]{0...) while((s32[]{:T(128)}, ...), condition=%wide.region_6.7_spmd, body=%wide.region_4.6_spmd.sunk | while | flops 430145792 | bytes 28231952 | solution.py:148
  211.2 2.0 fusion.135
  213.3 2.0 gather_fusion.3
  216.5 2.6 fusion.137
  219.1 1.4 fusion.138
  220.5 2.8 convolution_multiply_fusion.5
  223.4 2.2 copy.238
  225.6 3.8 fusion.140
  229.4 1.6 fusion.141
  231.0 3.8 fusion.142
  241.1 2.0 fusion.135
  243.1 2.0 gather_fusion.3
  245.1 1.2 fusion.136
  246.4 2.6 fusion.137
  249.0 1.4 fusion.138
  250.4 2.8 convolution_multiply_fusion.5
  253.2 2.2 copy.238
  255.5 3.8 fusion.140
  259.3 1.6 fusion.141
  260.9 3.8 fusion.142
  270.9 2.0 fusion.135
  273.0 2.0 gather_fusion.3
  275.0 1.2 fusion.136
  276.2 2.6 fusion.137
  278.8 1.4 fusion.138
  280.3 2.8 convolution_multiply_fusion.5
  283.1 2.2 copy.238
  285.4 3.8 fusion.140
  289.2 1.6 fusion.141
  290.8 3.8 fusion.142
  294.6 1.8 copy.181
  298.0 4.8 all-to-all-start.5
  305.1 5.8 all-to-all-done.5
  310.9 4.2 all-to-all-start.6
  315.1 569.4 %reduce-scatter.2.cloned.1.call-done = f32[192,24]{0,1:T(8,128)} async-done(((f32[192,1536]{0,1:T(8,128)}), f32[192,24]{0,1:T(8,128)}) %reduce-scatter.2.cloned.1.call-update) | async-done | bytes 18448 | tf_op jit(solution)/shard_map/reduce_scatter | solution.py:157
  884.5 1.3 broadcast_multiply_fusion
  885.8 9.5 %copy.226 = bf16[8,16,192,96]{3,1,2,0:T(8,128)(2,1)} copy(bf16[8,16,192,96]{3,2,1,0:T(8,128)(2,1)} %bitcast.245) | data formatting | bytes 9437184 | tf_op jit(solution)/shard_map/reshape | solution.py:118
  895.3 11.3 %dot_general.72 = bf16[1536,192,8]{0,1,2:T(8,128)(2,1)} reshape(bf16[16,96,192,8]{1,0,2,3:T(8,128)(2,1)} %bitcast.246) | data formatting | bytes 9437184 | tf_op jit(solution)/shard_map/tsr,sfrc->tfc/dot_general | solution.py:121
  908.9 16.3 %all-to-all-start.7 = ((bf16[8,128,192]{1,2,0:T(8,128)(2,1)}), bf16[8,128,192]{1,2,0:T(8,128)(2,1)S(1)}, u32[]{:S(2)}, u32[]{:S(2)}) async-start(bf16[8,128,192]{1,2,0:T(8,128)(2,1)} %copy.186), calls=%async_computation.7 | async-start | bytes 786432 | tf_op jit(solution)/shard_map/all_to_all | solution.py:152
  925.2 3.9 fusion.72
  930.9 2.3 all-to-all-done.7
  (175 shorter events, 53.3 us)
Async XLA Ops:
  7.2 13.0 %copy-start.6 = (bf16[1,128,1536]{2,1,0:T(8,128)(2,1)S(1)}, bf16[1,128,1536]{2,1,0:T(8,128)(2,1)}, u32[]{:S(2)}) copy-start(bf16[1,128,1536]{2,1,0:T(8,128)(2,1)} %param.12) | copy-start | bytes 1179652
  7.2 154.3 %all-gather.5.cloned.1.call-start = ((), (), s32[]{:S(2)}) async-start(), calls=%async_computation.10 | async-start | bytes 6340608 | tf_op jit(solution)/shard_map/all_gather | solution.py:117
  7.9 24.5 %copy-start.7 = (bf16[1,128,1536]{2,1,0:T(8,128)(2,1)S(1)}, bf16[1,128,1536]{2,1,0:T(8,128)(2,1)}, u32[]{:S(2)}) copy-start(bf16[1,128,1536]{2,1,0:T(8,128)(2,1)} %param.13) | copy-start | bytes 1179652
  9.9 18.3 %all-to-all-start = ((bf16[128,8,192]{0,2,1:T(8,128)(2,1)}), bf16[128,8,192]{0,2,1:T(8,128)(2,1)S(1)}, u32[]{:S(2)}, u32[]{:S(2)}) async-start(bf16[128,8,192]{0,2,1:T(8,128)(2,1)} %bitcast.31), calls=%async_computation | async-start | bytes 786432 | tf_op jit(solution)/shard_map/all_to_all | solution.py:89
  21.0 24.8 %copy-start.2 = (bf16[1,128,1536]{2,1,0:T(8,128)(2,1)S(1)}, bf16[1,128,1536]{2,1,0:T(8,128)(2,1)}, u32[]{:S(2)}) copy-start(bf16[1,128,1536]{2,1,0:T(8,128)(2,1)} %param.14) | copy-start | bytes 1179652
  28.2 12.8 %all-to-all-start.1 = ((bf16[128,8,192]{0,2,1:T(8,128)(2,1)}), bf16[128,8,192]{0,2,1:T(8,128)(2,1)S(1)}, u32[]{:S(2)}, u32[]{:S(2)}) async-start(bf16[128,8,192]{0,2,1:T(8,128)(2,1)} %bitcast.33), calls=%async_computation.1 | async-start | bytes 786432 | tf_op jit(solution)/shard_map/all_to_all | solution.py:90
  32.4 14.3 %copy-start.10 = (s32[1,3,32]{2,0,1:T(1,128)S(1)}, s32[1,3,32]{2,0,1:T(1,128)}, u32[]{:S(2)}) copy-start(s32[1,3,32]{2,0,1:T(1,128)} %param.17) | copy-start | bytes 1156
  32.4 14.3 %copy-start.8 = (s32[1,3,32,6]{2,0,3,1:T(1,128)S(1)}, s32[1,3,32,6]{2,0,3,1:T(1,128)}, u32[]{:S(2)}) copy-start(s32[1,3,32,6]{2,0,3,1:T(1,128)} %param.16) | copy-start | bytes 6916
  41.0 12.2 %all-to-all-start.2 = ((bf16[128,8,192]{0,2,1:T(8,128)(2,1)}), bf16[128,8,192]{0,2,1:T(8,128)(2,1)S(1)}, u32[]{:S(2)}, u32[]{:S(2)}) async-start(bf16[128,8,192]{0,2,1:T(8,128)(2,1)} %bitcast.35), calls=%async_computation.2 | async-start | bytes 786432 | tf_op jit(solution)/shard_map/all_to_all | solution.py:91
  45.1 148.9 %all-gather.7.cloned.1.call-start = ((), (), s32[]{:S(2)}) async-start(), calls=%async_computation.11 | async-start | bytes 3538944 | tf_op jit(solution)/shard_map/all_gather | solution.py:125
  86.9 2.5 copy-start.9
  170.8 10.7 %copy-start.3 = (bf16[1,128,1536]{1,2,0:T(8,128)(2,1)S(1)}, bf16[1,128,1536]{1,2,0:T(8,128)(2,1)}, u32[]{:S(2)}) copy-start(bf16[1,128,1536]{1,2,0:T(8,128)(2,1)} %copy.171) | copy-start | bytes 1179652
  185.7 12.8 %all-to-all-start.4 = ((bf16[128,8,192]{0,2,1:T(8,128)(2,1)}), bf16[128,8,192]{0,2,1:T(8,128)(2,1)S(1)}, u32[]{:S(2)}, u32[]{:S(2)}) async-start(bf16[128,8,192]{0,2,1:T(8,128)(2,1)} %bitcast.46), calls=%async_computation.4 | async-start | bytes 786432 | tf_op jit(solution)/shard_map/all_to_all | solution.py:133
  189.3 695.2 %reduce-scatter.2.cloned.1.call-start = ((), (), s32[]{:S(2)}) async-start(), calls=%async_computation.9 | async-start | bytes 1597440 | tf_op jit(solution)/shard_map/reduce_scatter | solution.py:157
  198.5 99.6 %all-to-all-start.3 = ((bf16[8,128,192]{1,2,0:T(8,128)(2,1)}), bf16[8,128,192]{1,2,0:T(8,128)(2,1)S(1)}, u32[]{:S(2)}, u32[]{:S(2)}) async-start(bf16[8,128,192]{1,2,0:T(8,128)(2,1)} %copy.169), calls=%async_computation.3 | async-start | bytes 786432 | tf_op jit(solution)/shard_map/all_to_all | solution.py:115
  205.0 2.5 copy-start.11
  213.2 3.3 copy-start
  225.6 3.8 copy-start.1
  231.0 3.8 copy-start.12
  234.8 2.5 copy-start.11
  243.1 3.3 copy-start
  255.5 3.8 copy-start.1
  260.9 3.8 copy-start.12
  264.7 2.5 copy-start.11
  273.0 3.3 copy-start
  285.4 3.8 copy-start.1
  290.8 3.8 copy-start.12
  296.4 6.4 copy-start.4
  298.0 12.9 %all-to-all-start.5 = ((bf16[8,128,192]{1,2,0:T(8,128)(2,1)}), bf16[8,128,192]{1,2,0:T(8,128)(2,1)S(1)}, u32[]{:S(2)}, u32[]{:S(2)}) async-start(bf16[8,128,192]{1,2,0:T(8,128)(2,1)} %copy.182), calls=%async_computation.5 | async-start | bytes 786432 | tf_op jit(solution)/shard_map/all_to_all | solution.py:150
  310.9 598.0 %all-to-all-start.6 = ((bf16[8,128,192]{1,2,0:T(8,128)(2,1)}), bf16[8,128,192]{1,2,0:T(8,128)(2,1)S(1)}, u32[]{:S(2)}, u32[]{:S(2)}) async-start(bf16[8,128,192]{1,2,0:T(8,128)(2,1)} %copy.184), calls=%async_computation.6 | async-start | bytes 786432 | tf_op jit(solution)/shard_map/all_to_all | solution.py:151
  895.3 11.3 %copy-start.5 = (bf16[3,32,32,64]{3,1,2,0:T(8,128)(2,1)S(1)}, bf16[3,32,32,64]{3,1,2,0:T(8,128)(2,1)}, u32[]{:S(2)}) copy-start(bf16[3,32,32,64]{3,1,2,0:T(8,128)(2,1)} %get-tuple-element.288) | copy-start | bytes 1179652
  908.9 24.3 %all-to-all-start.7 = ((bf16[8,128,192]{1,2,0:T(8,128)(2,1)}), bf16[8,128,192]{1,2,0:T(8,128)(2,1)S(1)}, u32[]{:S(2)}, u32[]{:S(2)}) async-start(bf16[8,128,192]{1,2,0:T(8,128)(2,1)} %copy.186), calls=%async_computation.7 | async-start | bytes 786432 | tf_op jit(solution)/shard_map/all_to_all | solution.py:152
Sparse Core Ops, SparseCore 0:
  11.1 150.2 all-gather.4
  163.6 30.3 all-gather.6
  198.6 685.8 reduce-scatter.1
where the time goes:
time: 944 us; the launch traced here: 941 us
  waiting for transfers between devices  672 us (71%)
  local copies, waits for them, and re-layouts  106 us (11%)
  matrix products  76.4 us (8%)
  starting transfers between devices  51.3 us (5%)
  between operations  14 us (1%)
  loops' own time  12.2 us (1%)
    reduce_scatter x1, waiting for transfers between devices, per_device(): lax.psum_scatter(weight_term, ('fsdp', 'dp'), scatter_dimension=1, tiled=...  569 us
    all_gather x1, waiting for transfers between devices, per_device(): lax.all_gather(out_weight[None], ('seq', 'fsdp'), axis=0, tiled=True)  70.4 us
  transfers between devices with their start and end apart: 11, of which 8 were waited for; matrix products, arithmetic and copies ran while one was open for 20% of the time, Pallas kernels for 0%

commit v1 on v0

--- a/solution.py
+++ b/solution.py
@@ -114,7 +114,12 @@
     attn_heads = heads_to_rows(attended)
     attn_tokens = lax.all_to_all(attn_heads, "seq", split_axis=0, concat_axis=1, tiled=True)
     row_block, col_block = out_weight.shape
-    gathered = lax.all_gather(out_weight[None], ("seq", "fsdp"), axis=0, tiled=True)
+    gathered = jnp.concatenate(
+        lax.all_to_all(
+            jnp.stack([out_weight[None]] * lax.axis_size(("seq", "fsdp"))), ("seq", "fsdp"), 0, 0
+        ),
+        axis=0,
+    )
     full_weight = gathered.reshape(seq_size, fsdp_size, row_block, col_block)
     weight_code = "sfrc"
     attn_split = attn_tokens.reshape(local_tokens, seq_size, row_block)

time: 944 us -> 1120 us (1.19)
  waiting for transfers between devices: 672 us -> 820 us
  blocking collectives: 0 us -> 11.3 us
    all_to_all x1, waiting for transfers between devices: 3.22 us -> 231 us  [per_device(): lax.all_to_all(jnp.stack([out_weight[None]] * lax.axis_size(('seq', 'fsdp...]
    all_gather x1 -> x0, waiting for transfers between devices: 70.4 us -> none  [per_device(): lax.all_gather(out_weight[None], ('seq', 'fsdp'), axis=0, tiled=True)]
    reshape x2 -> x0, local copies, waits for them, and re-layouts: 18.9 us -> none  [per_device(): full_weight = gathered.reshape(seq_size, fsdp_size, row_block, col_block)]
    all_to_all x0 -> x1, blocking collectives: none -> 11.3 us  [per_device(): lax.all_to_all(value_in[0], 'seq', split_axis=1, concat_axis=0, tiled=True)]
  transfers between devices with their start and end apart: 11 -> 10, of which waited for: 8 -> 7; matrix products, arithmetic and copies ran while one was open for 20% -> 17% of each run, Pallas kernels for 0% -> 0%
where the time goes in v1:
time: 1120 us
  waiting for transfers between devices  820 us (73%)
  local copies, waits for them, and re-layouts  110 us (10%)
  matrix products  76.4 us (7%)
  starting transfers between devices  62.2 us (6%)
  between operations  14.3 us (1%)
  loops' own time  12.2 us (1%)
  blocking collectives  11.3 us (1%)
    reduce_scatter x1, waiting for transfers between devices, per_device(): lax.psum_scatter(weight_term, ('fsdp', 'dp'), scatter_dimension=1, tiled=...  562 us
    all_to_all x1, waiting for transfers between devices, per_device(): lax.all_to_all(jnp.stack([out_weight[None]] * lax.axis_size(('seq', 'fsdp...  231 us
  transfers between devices with their start and end apart: 10, of which 7 were waited for; matrix products, arithmetic and copies ran while one was open for 17% of the time, Pallas kernels for 0%

profile of v1, /device:TPU:1, one launch (start us, length us, event | category | flops | bytes accessed | tf_op | source)
XLA Modules:
  0.0 1115.1 jit_solution(13883286424884009266)
XLA Ops:
  7.2 2.0 copy.157
  9.2 10.2 all-to-all-start
  20.3 7.2 all-to-all-done
  27.5 4.2 all-to-all-start.1
  32.0 7.9 all-to-all-done.1
  39.8 11.3 %all_to_all.133 = bf16[128,8,192]{0,2,1:T(8,128)(2,1)S(1)} all-to-all(bf16[128,8,192]{0,2,1:T(8,128)(2,1)S(1)} %bitcast.253), channel_id=1, replica_groups=mesh['seq'=8,'fsdp'=16,'dp'=4] {'seq'}, dimensions={1} | all-to-all | bytes 786432 | tf_op jit(solution)/shard_map/all_to_all | solution.py:91
  51.2 4.2 stack.3
  55.4 14.2 %all-to-all-start.4 = ((bf16[128,1,192,96]{3,2,1,0:T(8,128)(2,1)}), bf16[128,1,192,96]{3,2,1,0:T(8,128)(2,1)}, u32[]{:S(2)}, u32[]{:S(2)}) async-start(bf16[128,1,192,96]{3,2,1,0:T(8,128)(2,1)} %stack.3), calls=%async_computation.4 | async-start | bytes 12582912 | tf_op jit(solution)/shard_map/all_to_all | solution.py:118
  77.1 31.1 %while.30 = (s32[]{:T(128)}, bf16[3,32,32,64]{3,2,1,0:T(8,128)(2,1)}, f32[3,32,32,1]{2,1,3,0:T(8,128)}, s32[3]{0:T(128)S(1)}, s32[3,32]{1,0:T(4,128)S(1)}, /*ind...) while((s32[]{:T(128)}, ...), condition=%wide.region_3.4_spmd, body=%wide.region_0.3_spmd.sunk | while | flops 51781700 | bytes 8198467 | solution.py:113
  82.9 2.1 fusion.118
  86.0 1.5 fusion.119
  93.2 2.1 fusion.118
  96.3 1.5 fusion.119
  103.6 2.1 fusion.118
  106.7 1.5 fusion.119
  108.2 1.8 copy.167
  112.3 231.2 %all-to-all-done.4 = bf16[128,1,192,96]{3,2,1,0:T(8,128)(2,1)} async-done(((bf16[128,1,192,96]{3,2,1,0:T(8,128)(2,1)}), bf16[128,1,192,96]{3,2,1,0:T(8,128)(2,1)}, u32[]{:S(2)}, u32[]{:S(2)}) %all-to-all-start.4) | async-done | bytes 4718624 | tf_op jit(solution)/shard_map/all_to_all | solution.py:118
  343.5 9.4 copy.171
  352.9 10.6 dot_general.75
  363.5 3.1 fusion.71
  367.6 4.1 all-to-all-start.5
  371.7 4.4 fusion.68
  376.1 3.6 all-to-all-done.5
  379.8 4.2 all-to-all-start.3
  386.6 89.7 %while.31 = (s32[]{:T(128)}, bf16[3,32,32,64]{3,2,1,0:T(8,128)(2,1)}, bf16[3,32,32,64]{3,1,2,0:T(8,128)(2,1)}, bf16[3,32,32,64]{3,1,2,0:T(8,128)(2,1)}, s32[3]{0...) while((s32[]{:T(128)}, ...), condition=%wide.region_6.7_spmd, body=%wide.region_4.6_spmd.sunk | while | flops 430145792 | bytes 28231952 | solution.py:153
  392.9 2.0 fusion.135
  394.9 2.0 gather_fusion.3
  398.2 2.6 fusion.137
  400.8 1.4 fusion.138
  402.2 2.8 convolution_multiply_fusion.5
  405.0 2.2 copy.235
  407.3 3.8 fusion.140
  411.1 1.6 fusion.141
  412.7 3.8 fusion.142
  422.8 2.0 fusion.135
  424.8 2.0 gather_fusion.3
  428.1 2.6 fusion.137
  430.7 1.4 fusion.138
  432.1 2.8 convolution_multiply_fusion.5
  435.0 2.2 copy.235
  437.2 3.8 fusion.140
  441.0 1.6 fusion.141
  442.6 3.8 fusion.142
  452.7 2.0 fusion.135
  454.7 2.0 gather_fusion.3
  456.7 1.2 fusion.136
  458.0 2.6 fusion.137
  460.6 1.4 fusion.138
  462.0 2.8 convolution_multiply_fusion.5
  464.9 2.2 copy.235
  467.1 3.8 fusion.140
  471.0 1.6 fusion.141
  472.6 3.8 fusion.142
  476.3 1.8 copy.180
  479.8 4.8 all-to-all-start.6
  486.9 5.8 all-to-all-done.6
  492.7 4.2 all-to-all-start.7
  496.9 561.8 %reduce-scatter.2.cloned.1.call-done = f32[192,24]{0,1:T(8,128)} async-done(((f32[192,1536]{0,1:T(8,128)}), f32[192,24]{0,1:T(8,128)}) %reduce-scatter.2.cloned.1.call-update) | async-done | bytes 18448 | tf_op jit(solution)/shard_map/reduce_scatter | solution.py:162
  1058.7 1.3 broadcast_multiply_fusion
  1060.0 9.5 copy.169
  1069.5 11.3 %dot_general.72 = bf16[1536,192,8]{0,1,2:T(8,128)(2,1)} reshape(bf16[16,96,192,8]{1,0,2,3:T(8,128)(2,1)} %copy.169) | data formatting | bytes 9437184 | tf_op jit(solution)/shard_map/tsr,sfrc->tfc/dot_general | solution.py:126
  1083.1 16.2 %all-to-all-start.8 = ((bf16[8,128,192]{1,2,0:T(8,128)(2,1)}), bf16[8,128,192]{1,2,0:T(8,128)(2,1)S(1)}, u32[]{:S(2)}, u32[]{:S(2)}) async-start(bf16[8,128,192]{1,2,0:T(8,128)(2,1)} %copy.185), calls=%async_computation.8 | async-start | bytes 786432 | tf_op jit(solution)/shard_map/all_to_all | solution.py:157
  1099.2 3.9 fusion.72
  1105.0 2.3 all-to-all-done.8
  (176 shorter events, 53.2 us)
Async XLA Ops:
  7.2 12.2 %copy-start.6 = (bf16[1,128,1536]{2,1,0:T(8,128)(2,1)S(1)}, bf16[1,128,1536]{2,1,0:T(8,128)(2,1)}, u32[]{:S(2)}) copy-start(bf16[1,128,1536]{2,1,0:T(8,128)(2,1)} %param.12) | copy-start | bytes 1179652
  7.2 24.6 %copy-start.7 = (bf16[1,128,1536]{2,1,0:T(8,128)(2,1)S(1)}, bf16[1,128,1536]{2,1,0:T(8,128)(2,1)}, u32[]{:S(2)}) copy-start(bf16[1,128,1536]{2,1,0:T(8,128)(2,1)} %param.13) | copy-start | bytes 1179652
  9.2 18.3 %all-to-all-start = ((bf16[128,8,192]{0,2,1:T(8,128)(2,1)}), bf16[128,8,192]{0,2,1:T(8,128)(2,1)S(1)}, u32[]{:S(2)}, u32[]{:S(2)}) async-start(bf16[128,8,192]{0,2,1:T(8,128)(2,1)} %bitcast.31), calls=%async_computation | async-start | bytes 786432 | tf_op jit(solution)/shard_map/all_to_all | solution.py:89
  19.4 31.7 %copy-start.8 = (bf16[192,96]{1,0:T(8,128)(2,1)S(1)}, bf16[192,96]{1,0:T(8,128)(2,1)}, u32[]{:S(2)}) copy-start(bf16[192,96]{1,0:T(8,128)(2,1)} %param.15) | copy-start | bytes 110596
  27.5 12.3 %all-to-all-start.1 = ((bf16[128,8,192]{0,2,1:T(8,128)(2,1)}), bf16[128,8,192]{0,2,1:T(8,128)(2,1)S(1)}, u32[]{:S(2)}, u32[]{:S(2)}) async-start(bf16[128,8,192]{0,2,1:T(8,128)(2,1)} %bitcast.33), calls=%async_computation.1 | async-start | bytes 786432 | tf_op jit(solution)/shard_map/all_to_all | solution.py:90
  55.3 14.9 %copy-start.2 = (bf16[1,128,1536]{2,1,0:T(8,128)(2,1)S(1)}, bf16[1,128,1536]{2,1,0:T(8,128)(2,1)}, u32[]{:S(2)}) copy-start(bf16[1,128,1536]{2,1,0:T(8,128)(2,1)} %param.14) | copy-start | bytes 1179652
  55.3 15.9 %copy-start.11 = (s32[1,3,32]{2,0,1:T(1,128)S(1)}, s32[1,3,32]{2,0,1:T(1,128)}, u32[]{:S(2)}) copy-start(s32[1,3,32]{2,0,1:T(1,128)} %param.17) | copy-start | bytes 1156
  55.3 15.9 %copy-start.9 = (s32[1,3,32,6]{2,0,3,1:T(1,128)S(1)}, s32[1,3,32,6]{2,0,3,1:T(1,128)}, u32[]{:S(2)}) copy-start(s32[1,3,32,6]{2,0,3,1:T(1,128)} %param.16) | copy-start | bytes 6916
  55.4 288.2 %all-to-all-start.4 = ((bf16[128,1,192,96]{3,2,1,0:T(8,128)(2,1)}), bf16[128,1,192,96]{3,2,1,0:T(8,128)(2,1)}, u32[]{:S(2)}, u32[]{:S(2)}) async-start(bf16[128,1,192,96]{3,2,1,0:T(8,128)(2,1)} %stack.3), calls=%async_computation.4 | async-start | bytes 12582912 | tf_op jit(solution)/shard_map/all_to_all | solution.py:118
  69.5 302.2 %all-gather.3.cloned.1.call-start = ((), (), s32[]{:S(2)}) async-start(), calls=%async_computation.11 | async-start | bytes 3538944 | tf_op jit(solution)/shard_map/all_gather | solution.py:130
  108.2 2.5 copy-start.10
  352.9 10.6 copy-start.3
  367.6 12.2 %all-to-all-start.5 = ((bf16[128,8,192]{0,2,1:T(8,128)(2,1)}), bf16[128,8,192]{0,2,1:T(8,128)(2,1)S(1)}, u32[]{:S(2)}, u32[]{:S(2)}) async-start(bf16[128,8,192]{0,2,1:T(8,128)(2,1)} %bitcast.46), calls=%async_computation.5 | async-start | bytes 786432 | tf_op jit(solution)/shard_map/all_to_all | solution.py:138
  371.7 687.0 %reduce-scatter.2.cloned.1.call-start = ((), (), s32[]{:S(2)}) async-start(), calls=%async_computation.10 | async-start | bytes 1597440 | tf_op jit(solution)/shard_map/reduce_scatter | solution.py:162
  379.8 100.0 %all-to-all-start.3 = ((bf16[8,128,192]{1,2,0:T(8,128)(2,1)}), bf16[8,128,192]{1,2,0:T(8,128)(2,1)S(1)}, u32[]{:S(2)}, u32[]{:S(2)}) async-start(bf16[8,128,192]{1,2,0:T(8,128)(2,1)} %copy.168), calls=%async_computation.3 | async-start | bytes 786432 | tf_op jit(solution)/shard_map/all_to_all | solution.py:115
  386.6 2.5 copy-start.12
  394.9 3.3 copy-start
  407.3 3.8 copy-start.1
  412.7 3.8 copy-start.13
  416.5 2.5 copy-start.12
  424.8 3.3 copy-start
  437.2 3.8 copy-start.1
  442.6 3.8 copy-start.13
  446.4 2.5 copy-start.12
  454.7 3.3 copy-start
  467.1 3.8 copy-start.1
  472.6 3.8 copy-start.13
  478.2 6.4 copy-start.4
  479.8 12.9 %all-to-all-start.6 = ((bf16[8,128,192]{1,2,0:T(8,128)(2,1)}), bf16[8,128,192]{1,2,0:T(8,128)(2,1)S(1)}, u32[]{:S(2)}, u32[]{:S(2)}) async-start(bf16[8,128,192]{1,2,0:T(8,128)(2,1)} %copy.181), calls=%async_computation.6 | async-start | bytes 786432 | tf_op jit(solution)/shard_map/all_to_all | solution.py:155
  492.7 590.4 %all-to-all-start.7 = ((bf16[8,128,192]{1,2,0:T(8,128)(2,1)}), bf16[8,128,192]{1,2,0:T(8,128)(2,1)S(1)}, u32[]{:S(2)}, u32[]{:S(2)}) async-start(bf16[8,128,192]{1,2,0:T(8,128)(2,1)} %copy.183), calls=%async_computation.7 | async-start | bytes 786432 | tf_op jit(solution)/shard_map/all_to_all | solution.py:156
  1069.5 11.3 %copy-start.5 = (bf16[3,32,32,64]{3,1,2,0:T(8,128)(2,1)S(1)}, bf16[3,32,32,64]{3,1,2,0:T(8,128)(2,1)}, u32[]{:S(2)}) copy-start(bf16[3,32,32,64]{3,1,2,0:T(8,128)(2,1)} %get-tuple-element.288) | copy-start | bytes 1179652
  1083.1 24.3 %all-to-all-start.8 = ((bf16[8,128,192]{1,2,0:T(8,128)(2,1)}), bf16[8,128,192]{1,2,0:T(8,128)(2,1)S(1)}, u32[]{:S(2)}, u32[]{:S(2)}) async-start(bf16[8,128,192]{1,2,0:T(8,128)(2,1)} %copy.185), calls=%async_computation.8 | async-start | bytes 786432 | tf_op jit(solution)/shard_map/all_to_all | solution.py:157
Sparse Core Ops, SparseCore 0:
  72.5 41.3 all-gather.2
  376.9 681.7 reduce-scatter.1
